TPU v7x, 32 devices: a whole 2x2x4 slice. The times are simulated.
32 devices in a mesh: grp: 4 (over y, core), row: 8 (over z, x).
Axes of the slice: x: 2, y: 2, z: 4, core: 2. Of those that a mesh axis runs over, the one named last changes fastest.
Arguments:
- a_blocks: bfloat16 [81920, 512], P(('grp', 'row')), may hold values from -0.25 to 0.25
- a_cols: int32 [1280, 8], P(('grp', 'row')), may hold values from 0 to 1279, as said below
- a_count: int32 [1280], P(('grp', 'row')), may hold values from 2 to 8, as said below
- p_blocks: bfloat16 [81920, 256], P(('grp', 'row')), may hold values from -0.75 to 0.75
- p_cols: int32 [1280, 4], P(('grp', 'row')), may hold values from 0 to 319, as said below
- q2_blocks: bfloat16 [320, 4096], P(('grp', 'row')), may hold values from -0.75 to 0.75
- agg3: int32 [320], P(('grp', 'row')), may hold values from 0 to 47, as said below
Outputs:
- level2_op: bfloat16 [20480, 3200], P(('grp', 'row'))
- level3_op: float32 [3072, 2304], P('grp')
Inputs may be any that keep to these rules, and one draw needn't show every extreme that they name: a_cols[i, 0] = i, and every a_cols[i, k] differs from i by at most 40. `a_count`: block rows i with i % 40 == 0 use all 8 blocks. `p_cols`: the 4 entries of a row are distinct and lie from 10 (i // 40) to 10 (i // 40 + 2) - 1 for block row i. agg3[c] lies from 12 g to 12 (g + 1) - 1 with g = c // 80.
All inputs are finite; a program needn't handle non-finite values.
Results may differ from a plain program's by a relative error of at most 0.0058.
Values may be sent and summed in bfloat16 or wider, within the bound.
A program may use at most 128 MiB of HBM per device.

v0:
```python
import jax
import jax.numpy as jnp
from jax import lax
from jax.sharding import PartitionSpec as P

B = 64
KA = 8
KP = 4
A3G = 12


def padded(array, sides, width):
    for axis, dim in sides:
        devices, length = (lax.axis_size(axis), array.shape[dim])
        up = [(i, (i + 1) % devices) for i in range(devices - 1)]
        down = [(j, i) for i, j in up]
        last = lax.slice_in_dim(array, length - width, length, axis=dim)
        leading = lax.slice_in_dim(array, 0, width, axis=dim)
        before = lax.ppermute(last, axis, up)
        after = lax.ppermute(leading, axis, down)
        array = jnp.concatenate([before, array, after], axis=dim)
    return array


def passed_along(array, axis, by):
    devices = lax.axis_size(axis)
    pairs = [(i, i + by) for i in range(devices) if 0 <= i + by < devices]
    return lax.ppermute(array, axis, pairs)


def per_device(a_blocks, a_cols, a_count, p_blocks, p_cols, q2_blocks, agg3):
    highest_precision_flag = lax.Precision.HIGHEST
    rows_dev = a_cols.shape[0]
    coarse_dev = q2_blocks.shape[0]
    band = coarse_dev * B
    device = lax.axis_index(("grp", "row"))
    row_size = lax.axis_size("row")
    group = device // row_size
    ext_p = padded(p_blocks, ((("grp", "row"), 0),), rows_dev * B)
    ext_cols = padded(p_cols, ((("grp", "row"), 0),), rows_dev)
    ext_p = ext_p.reshape(3 * rows_dev, B, KP * B)
    turns = rows_dev // 4
    blk_a = a_blocks.reshape(turns, 4, B, KA, B)
    blk_cols = a_cols.reshape(turns, 4, KA)
    blk_count = a_count.reshape(turns, 4)
    blk_p = p_blocks.reshape(turns, 4, B, KP, B)
    blk_pc = p_cols.reshape(turns, 4, KP)
    wide_ids = jnp.arange(4 * coarse_dev, dtype=jnp.int32)
    own_ids = jnp.arange(2 * coarse_dev, dtype=jnp.int32)
    slots = jnp.arange(KA, dtype=jnp.int32)

    def accumulate_block_entry(total, pieces):
        amat, cols, count, pmat, pcols = pieces
        keep = slots[None, :] < count[:, None]
        amat = jnp.where(keep[:, None, :, None], amat, jnp.zeros_like(amat))
        local = cols - (device - 1) * rows_dev
        prow = ext_p[local]
        pattern = ext_cols[local] - (device - 1) * coarse_dev
        hot = (pattern[..., None] == wide_ids).astype(jnp.float32)
        prod = jnp.einsum("rfkg,rkgq->rkfq", amat, prow, preferred_element_type=jnp.float32)
        prod = prod.reshape(prod.shape[0], KA, B, KP, B)
        wide = jnp.einsum("rkfmq,rkmc->rfcq", prod, hot, precision=highest_precision_flag).astype(
            jnp.bfloat16
        )
        wide = wide.reshape(wide.shape[0], B, 4 * band)
        part = jnp.einsum("rfmq,rfx->rmqx", pmat, wide, preferred_element_type=jnp.float32)
        owner_hot = ((pcols - device * coarse_dev)[..., None] == own_ids).astype(jnp.float32)
        return (
            total + jnp.einsum("rmt,rmqx->tqx", owner_hot, part, precision=highest_precision_flag),
            None,
        )

    start = jnp.zeros((2 * coarse_dev, B, 4 * band), jnp.float32)
    total, unused = lax.scan(
        accumulate_block_entry, start, (blk_a, blk_cols, blk_count, blk_p, blk_pc)
    )
    total = total.reshape(2 * band, 4 * band)
    sent = passed_along(total[band:], ("grp", "row"), 1)
    level2 = jnp.pad(total[:band], ((0, 0), (band, 0))) + jnp.pad(sent, ((0, 0), (0, band)))
    coarse = level2.astype(jnp.bfloat16)
    near_q = padded(q2_blocks, ((("grp", "row"), 0),), coarse_dev)
    near_agg = padded(agg3, ((("grp", "row"), 0),), coarse_dev)
    lower_q = passed_along(q2_blocks, ("grp", "row"), 2)
    lower_agg = passed_along(agg3, ("grp", "row"), 2)
    upper_q = passed_along(q2_blocks, ("grp", "row"), -2)
    upper_agg = passed_along(agg3, ("grp", "row"), -2)
    ext_q = jnp.concatenate([lower_q, near_q, upper_q], axis=0)
    ext_agg = jnp.concatenate([lower_agg, near_agg, upper_agg], axis=0)
    ext_q = ext_q.reshape(5 * coarse_dev, B, B)
    slot_ids = jnp.arange(3 * A3G, dtype=jnp.int32)
    block_position = ((ext_agg - (group - 1) * A3G)[:, None] == slot_ids).astype(jnp.float32)
    coarse_three = coarse.reshape(band, 5 * coarse_dev, B)
    galerkin_triple_products = jnp.einsum(
        "rjp,jpq->rjq", coarse_three, ext_q, preferred_element_type=jnp.float32
    )
    mixed_precision_result = jnp.einsum(
        "ead,ao->eod", galerkin_triple_products, block_position, precision=highest_precision_flag
    ).astype(jnp.bfloat16)
    mixed_precision_result = mixed_precision_result.reshape(coarse_dev, B, 3 * A3G * B)
    blocks_q = q2_blocks.reshape(coarse_dev, B, B)
    terms = jnp.einsum(
        "cpq,cpx->cqx", blocks_q, mixed_precision_result, preferred_element_type=jnp.float32
    )
    own_hot = ((agg3 - group * A3G)[:, None] == jnp.arange(A3G, dtype=jnp.int32)).astype(
        jnp.float32
    )
    share_sum = jnp.einsum("ca,cqx->aqx", own_hot, terms, precision=highest_precision_flag).reshape(
        A3G * B, 3 * A3G * B
    )
    level3 = lax.psum(share_sum, "row")
    return (coarse, level3)


def solution(mesh):
    in_specs = (
        P(("grp", "row"), None),
        P(("grp", "row"), None),
        P(("grp", "row")),
        P(("grp", "row"), None),
        P(("grp", "row"), None),
        P(("grp", "row"), None),
        P(("grp", "row")),
    )
    out_specs = (P(("grp", "row"), None), P("grp", None))
    return jax.shard_map(
        per_device, mesh=mesh, in_specs=in_specs, out_specs=out_specs, check_vma=False
    )
```

profile of v0, /device:TPU:0, one launch (start us, length us, event | category | flops | bytes accessed | tf_op | source)
XLA Modules:
  0.0 1156.5 jit_solution(13000389786499118153)
XLA Ops:
  28.2 7.5 reshape.161
  35.7 33.7 %collective-permute-done.1 = s32[40,4]{0,1:T(4,128)S(1)} collective-permute-done((s32[40,4]{0,1:T(4,128)}, s32[40,4]{0,1:T(4,128)S(1)}, u32[]{:S(2)}, u32[]{:S(2)}) %collective-permute-start.1) | collective-permute-done | bytes 672 | tf_op jit(solution)/shard_map/ppermute | solution.py:20
  72.8 561.9 %while.13 = (s32[]{:T(128)}, f32[20,64,2560]{2,0,1:T(8,128)}, s32[10,4,4]{2,1,0:T(4,128)S(1)}, s32[]{:T(128)}, bf16[10,4,64,4,64]{4,3,2,1,0:T(4,128)(2,1)}, /*in...) while((s32[]{:T(128)}, f32[20,64,2560]{2,0,1:T(8,128)}, ...), condition=%wide.region_1.2_spmd.clone, body=%wide.region_0.1_spmd.clone.sunk | while | flops 1290803712 | bytes 65414116 | solution.py:74
  99.4 27.7 %bitcast_add_fusion.2 = f32[20,64,2560]{2,0,1:T(8,128)} fusion(f32[20,64,2560]{2,0,1:T(8,128)} %get-tuple-element.385, pred[]{:T(512)S(6)} %compare.7, f32[4,4,64,2560]{3,2,1,0:T(8,128)} %fusion.75, s32[4,4]{0,1:T(4,128)S(1)} %copy.153), kind=kOutput, calls=%fused_computation.5.clone.1 | convolution fusion | flops 635699520 | bytes 36700224 | tf_op jit(solution)/shard_map/while/body/eval_jaxpr/rmt,rmqx->tqx/dot_general | solution.py:69
  135.3 7.4 fusion.74
  153.4 30.0 %bitcast_add_fusion.2 = f32[20,64,2560]{2,0,1:T(8,128)} fusion(f32[20,64,2560]{2,0,1:T(8,128)} %get-tuple-element.385, pred[]{:T(512)S(6)} %compare.7, f32[4,4,64,2560]{3,2,1,0:T(8,128)} %fusion.75, s32[4,4]{0,1:T(4,128)S(1)} %copy.153), kind=kOutput, calls=%fused_computation.5.clone.1 | convolution fusion | flops 635699520 | bytes 36700224 | tf_op jit(solution)/shard_map/while/body/eval_jaxpr/rmt,rmqx->tqx/dot_general | solution.py:69
  209.8 30.0 %bitcast_add_fusion.2 = f32[20,64,2560]{2,0,1:T(8,128)} fusion(f32[20,64,2560]{2,0,1:T(8,128)} %get-tuple-element.385, pred[]{:T(512)S(6)} %compare.7, f32[4,4,64,2560]{3,2,1,0:T(8,128)} %fusion.75, s32[4,4]{0,1:T(4,128)S(1)} %copy.153), kind=kOutput, calls=%fused_computation.5.clone.1 | convolution fusion | flops 635699520 | bytes 36700224 | tf_op jit(solution)/shard_map/while/body/eval_jaxpr/rmt,rmqx->tqx/dot_general | solution.py:69
  266.1 30.0 %bitcast_add_fusion.2 = f32[20,64,2560]{2,0,1:T(8,128)} fusion(f32[20,64,2560]{2,0,1:T(8,128)} %get-tuple-element.385, pred[]{:T(512)S(6)} %compare.7, f32[4,4,64,2560]{3,2,1,0:T(8,128)} %fusion.75, s32[4,4]{0,1:T(4,128)S(1)} %copy.153), kind=kOutput, calls=%fused_computation.5.clone.1 | convolution fusion | flops 635699520 | bytes 36700224 | tf_op jit(solution)/shard_map/while/body/eval_jaxpr/rmt,rmqx->tqx/dot_general | solution.py:69
  304.4 7.4 fusion.74
  322.5 30.0 %bitcast_add_fusion.2 = f32[20,64,2560]{2,0,1:T(8,128)} fusion(f32[20,64,2560]{2,0,1:T(8,128)} %get-tuple-element.385, pred[]{:T(512)S(6)} %compare.7, f32[4,4,64,2560]{3,2,1,0:T(8,128)} %fusion.75, s32[4,4]{0,1:T(4,128)S(1)} %copy.153), kind=kOutput, calls=%fused_computation.5.clone.1 | convolution fusion | flops 635699520 | bytes 36700224 | tf_op jit(solution)/shard_map/while/body/eval_jaxpr/rmt,rmqx->tqx/dot_general | solution.py:69
  378.8 30.0 %bitcast_add_fusion.2 = f32[20,64,2560]{2,0,1:T(8,128)} fusion(f32[20,64,2560]{2,0,1:T(8,128)} %get-tuple-element.385, pred[]{:T(512)S(6)} %compare.7, f32[4,4,64,2560]{3,2,1,0:T(8,128)} %fusion.75, s32[4,4]{0,1:T(4,128)S(1)} %copy.153), kind=kOutput, calls=%fused_computation.5.clone.1 | convolution fusion | flops 635699520 | bytes 36700224 | tf_op jit(solution)/shard_map/while/body/eval_jaxpr/rmt,rmqx->tqx/dot_general | solution.py:69
  435.2 30.0 %bitcast_add_fusion.2 = f32[20,64,2560]{2,0,1:T(8,128)} fusion(f32[20,64,2560]{2,0,1:T(8,128)} %get-tuple-element.385, pred[]{:T(512)S(6)} %compare.7, f32[4,4,64,2560]{3,2,1,0:T(8,128)} %fusion.75, s32[4,4]{0,1:T(4,128)S(1)} %copy.153), kind=kOutput, calls=%fused_computation.5.clone.1 | convolution fusion | flops 635699520 | bytes 36700224 | tf_op jit(solution)/shard_map/while/body/eval_jaxpr/rmt,rmqx->tqx/dot_general | solution.py:69
  491.6 30.0 %bitcast_add_fusion.2 = f32[20,64,2560]{2,0,1:T(8,128)} fusion(f32[20,64,2560]{2,0,1:T(8,128)} %get-tuple-element.385, pred[]{:T(512)S(6)} %compare.7, f32[4,4,64,2560]{3,2,1,0:T(8,128)} %fusion.75, s32[4,4]{0,1:T(4,128)S(1)} %copy.153), kind=kOutput, calls=%fused_computation.5.clone.1 | convolution fusion | flops 635699520 | bytes 36700224 | tf_op jit(solution)/shard_map/while/body/eval_jaxpr/rmt,rmqx->tqx/dot_general | solution.py:69
  529.9 7.4 fusion.74
  547.9 30.0 %bitcast_add_fusion.2 = f32[20,64,2560]{2,0,1:T(8,128)} fusion(f32[20,64,2560]{2,0,1:T(8,128)} %get-tuple-element.385, pred[]{:T(512)S(6)} %compare.7, f32[4,4,64,2560]{3,2,1,0:T(8,128)} %fusion.75, s32[4,4]{0,1:T(4,128)S(1)} %copy.153), kind=kOutput, calls=%fused_computation.5.clone.1 | convolution fusion | flops 635699520 | bytes 36700224 | tf_op jit(solution)/shard_map/while/body/eval_jaxpr/rmt,rmqx->tqx/dot_general | solution.py:69
  604.3 30.0 %bitcast_add_fusion.2 = f32[20,64,2560]{2,0,1:T(8,128)} fusion(f32[20,64,2560]{2,0,1:T(8,128)} %get-tuple-element.385, pred[]{:T(512)S(6)} %compare.7, f32[4,4,64,2560]{3,2,1,0:T(8,128)} %fusion.75, s32[4,4]{0,1:T(4,128)S(1)} %copy.153), kind=kOutput, calls=%fused_computation.5.clone.1 | convolution fusion | flops 635699520 | bytes 36700224 | tf_op jit(solution)/shard_map/while/body/eval_jaxpr/rmt,rmqx->tqx/dot_general | solution.py:69
  634.7 17.8 %copy.104 = f32[20,64,2560]{2,1,0:T(8,128)} copy(f32[20,64,2560]{2,0,1:T(8,128)} %get-tuple-element.163) | data formatting | bytes 26214400 | tf_op jit(solution)/shard_map/while | solution.py:74
  652.5 11.2 fusion.43
  683.2 133.9 %collective-permute-start.6 = (s32[10]{0:T(128)S(1)}, s32[10]{0:T(128)S(1)}, u32[]{:S(2)}, u32[]{:S(2)}) collective-permute-start(s32[10]{0:T(128)S(1)} %copy-done.3), channel_id=1, source_target_pairs={{0,1},{1,2},{2,3},{3,4},{4,5},{5,6},{6,7},{7,8},{8,9},{9,10},{10,1... | collective-permute-start | bytes 128 | tf_op jit(solution)/shard_map/ppermute | solution.py:19
  857.4 8.3 convert_bitcast_fusion
  865.7 12.2 %copy.109 = bf16[640,36,64]{2,1,0:T(8,128)(2,1)} copy(bf16[640,36,64]{0,1,2:T(8,128)(2,1)S(1)} %convert_bitcast_fusion) | data formatting | bytes 5898240 | tf_op jit(solution)/shard_map/convert_element_type | solution.py:98
  877.9 8.2 reshape.165
  887.1 8.1 fusion.31
  902.3 240.7 %all-reduce.4.cloned.1.call-done = f32[768,2304]{1,0:T(8,128)} async-done(((f32[768,2304]{1,0:T(8,128)}), f32[768,2304]{1,0:T(8,128)}) %all-reduce.4.cloned.1.call-update) | async-done | bytes 7077904 | tf_op jit(solution)/shard_map/psum | solution.py:110
  (241 shorter events, 339.2 us)
Async XLA Ops:
  7.2 62.5 %copy-start = (bf16[2560,256]{1,0:T(8,128)(2,1)S(1)}, bf16[2560,256]{1,0:T(8,128)(2,1)}, u32[]{:S(2)}) copy-start(bf16[2560,256]{1,0:T(8,128)(2,1)} %param.12) | copy-start | bytes 3932164
  7.2 62.3 %copy-start.2 = (s32[40,4]{0,1:T(4,128)S(1)}, s32[40,4]{0,1:T(4,128)}, u32[]{:S(2)}) copy-start(s32[40,4]{0,1:T(4,128)} %param.13) | copy-start | bytes 1924
  7.2 1135.8 %all-reduce.4.cloned.1.call-start = ((), (), s32[]{:S(2)}) async-start(), calls=%async_computation | async-start | bytes 14155776 | tf_op jit(solution)/shard_map/psum | solution.py:110
  7.2 62.4 %collective-permute-start.3 = (bf16[2560,256]{1,0:T(8,128)(2,1)}, bf16[2560,256]{1,0:T(8,128)(2,1)S(1)}, u32[]{:S(2)}, u32[]{:S(2)}) collective-permute-start(bf16[2560,256]{1,0:T(8,128)(2,1)} %param.12), channel_id=1, source_target_pairs={{1,0},{2,1},{3,2},{4,3},{5,4},{6,5},{7,6},{8,7},{9,8},{10,9},{11,1... | collective-permute-start | bytes 3932168 | tf_op jit(solution)/shard_map/ppermute | solution.py:20
  8.7 61.0 %collective-permute-start.2 = (bf16[2560,256]{1,0:T(8,128)(2,1)}, bf16[2560,256]{1,0:T(8,128)(2,1)}, u32[]{:S(2)}, u32[]{:S(2)}) collective-permute-start(bf16[2560,256]{1,0:T(8,128)(2,1)} %param.12), channel_id=1, source_target_pairs={{0,1},{1,2},{2,3},{3,4},{4,5},{5,6},{6,7},{7,8},{8,9},{9,10},{10,1... | collective-permute-start | bytes 3932168 | tf_op jit(solution)/shard_map/ppermute | solution.py:19
  15.2 54.2 %collective-permute-start.1 = (s32[40,4]{0,1:T(4,128)}, s32[40,4]{0,1:T(4,128)S(1)}, u32[]{:S(2)}, u32[]{:S(2)}) collective-permute-start(s32[40,4]{0,1:T(4,128)} %param.13), channel_id=1, source_target_pairs={{1,0},{2,1},{3,2},{4,3},{5,4},{6,5},{7,6},{8,7},{9,8},{10,9},{11,1... | collective-permute-start | bytes 1928 | tf_op jit(solution)/shard_map/ppermute | solution.py:20
  16.5 53.0 %collective-permute-start = (s32[40,4]{0,1:T(4,128)}, s32[40,4]{0,1:T(4,128)S(1)}, u32[]{:S(2)}, u32[]{:S(2)}) collective-permute-start(s32[40,4]{0,1:T(4,128)} %param.13), channel_id=1, source_target_pairs={{0,1},{1,2},{2,3},{3,4},{4,5},{5,6},{6,7},{7,8},{8,9},{9,10},{10,1... | collective-permute-start | bytes 1928 | tf_op jit(solution)/shard_map/ppermute | solution.py:19
  652.5 18.3 %copy-start.1 = (bf16[10,4096]{1,0:T(8,128)(2,1)S(1)}, bf16[10,4096]{1,0:T(8,128)(2,1)}, u32[]{:S(2)}) copy-start(bf16[10,4096]{1,0:T(8,128)(2,1)} %param.14) | copy-start | bytes 245764
  652.5 23.0 %copy-start.3 = (s32[10]{0:T(128)S(1)}, s32[10]{0:T(128)}, u32[]{:S(2)}) copy-start(s32[10]{0:T(128)} %param.15) | copy-start | bytes 124
  663.7 176.1 %collective-permute-start.4 = (f32[640,2560]{1,0:T(8,128)}, f32[640,2560]{1,0:T(8,128)}, u32[]{:S(2)}, u32[]{:S(2)}) collective-permute-start(f32[640,2560]{1,0:T(8,128)} %bitcast.102), channel_id=1, source_target_pairs={{0,1},{1,2},{2,3},{3,4},{4,5},{5,6},{6,7},{7,8},{8,9},{9,10},{10,1... | collective-permute-start | bytes 19660808 | tf_op jit(solution)/shard_map/ppermute | solution.py:28
  670.8 160.4 %collective-permute-start.9 = (bf16[10,4096]{1,0:T(8,128)(2,1)S(1)}, bf16[10,4096]{1,0:T(8,128)(2,1)S(1)}, u32[]{:S(2)}, u32[]{:S(2)}) collective-permute-start(bf16[10,4096]{1,0:T(8,128)(2,1)S(1)} %copy-done.1), channel_id=1, source_target_pairs={{0,2},{1,3},{2,4},{3,5},{4,6},{5,7},{6,8},{7,9},{8,10},{9,11},{10,... | collective-permute-start | bytes 245768 | tf_op jit(solution)/shard_map/ppermute | solution.py:28
  672.1 159.1 %collective-permute-start.10 = (bf16[10,4096]{1,0:T(8,128)(2,1)S(1)}, bf16[10,4096]{1,0:T(8,128)(2,1)S(1)}, u32[]{:S(2)}, u32[]{:S(2)}) collective-permute-start(bf16[10,4096]{1,0:T(8,128)(2,1)S(1)} %copy-done.1), channel_id=1, source_target_pairs={{0,1},{1,2},{2,3},{3,4},{4,5},{5,6},{6,7},{7,8},{8,9},{9,10},{10,1... | collective-permute-start | bytes 245768 | tf_op jit(solution)/shard_map/ppermute | solution.py:19
  674.2 157.1 %collective-permute-start.11 = (bf16[10,4096]{1,0:T(8,128)(2,1)S(1)}, bf16[10,4096]{1,0:T(8,128)(2,1)S(1)}, u32[]{:S(2)}, u32[]{:S(2)}) collective-permute-start(bf16[10,4096]{1,0:T(8,128)(2,1)S(1)} %copy-done.1), channel_id=1, source_target_pairs={{1,0},{2,1},{3,2},{4,3},{5,4},{6,5},{7,6},{8,7},{9,8},{10,9},{11,1... | collective-permute-start | bytes 245768 | tf_op jit(solution)/shard_map/ppermute | solution.py:20
  675.5 7.7 collective-permute-start.5
  683.2 135.2 %collective-permute-start.6 = (s32[10]{0:T(128)S(1)}, s32[10]{0:T(128)S(1)}, u32[]{:S(2)}, u32[]{:S(2)}) collective-permute-start(s32[10]{0:T(128)S(1)} %copy-done.3), channel_id=1, source_target_pairs={{0,1},{1,2},{2,3},{3,4},{4,5},{5,6},{6,7},{7,8},{8,9},{9,10},{10,1... | collective-permute-start | bytes 128 | tf_op jit(solution)/shard_map/ppermute | solution.py:19
  818.4 5.7 collective-permute-start.7
  824.0 5.8 collective-permute-start.8
  829.8 7.9 collective-permute-start.12
Sparse Core Ops, SparseCore 0:
  902.4 240.5 all-reduce.3
where the time goes:
time: 1160 us
  matrix products  466 us (40%)
  waiting for transfers between devices  292 us (25%)
  local copies, waits for them, and re-layouts  201 us (17%)
  starting transfers between devices  170 us (15%)
  between operations  14.5 us (1%)
  other arithmetic  11.6 us (1%)
    dot_general x10, matrix products, accumulate_block_entry(): jnp.einsum('rmt,rmqx->tqx', owner_hot, part, precision=highest_precision_...  298 us
    psum x1, waiting for transfers between devices, per_device(): level3 = lax.psum(share_sum, 'row')  241 us
    ppermute x4, starting transfers between devices, padded(): before = lax.ppermute(last, axis, up)  147 us
    dot_general x10, matrix products, accumulate_block_entry(): jnp.einsum('rkfmq,rkmc->rfcq', prod, hot, precision=highest_precision_flag)  74.3 us
    dot_general x10, matrix products, accumulate_block_entry(): jnp.einsum('rfmq,rfx->rmqx', pmat, wide, preferred_element_type=jnp.float32)  67.9 us
    ppermute x4, waiting for transfers between devices, padded(): after = lax.ppermute(leading, axis, down)  38.1 us
    reshape x10, local copies, waits for them, and re-layouts, accumulate_block_entry(): prod = prod.reshape(prod.shape[0], KA, B, KP, B)  30.8 us
    gather x10, local copies, waits for them, and re-layouts, accumulate_block_entry(): prow = ext_p[local]  27.3 us
  transfers between devices with their start and end apart: 14, of which 8 were waited for; matrix products, arithmetic and copies ran while one was open for 1% of the time, Pallas kernels for 0%

commit v1 on v0

v1 whole, which is shorter than its diff:
```python
import functools

import jax
import jax.numpy as jnp
from jax import lax
from jax.experimental import pallas as pl
from jax.experimental.pallas import tpu as pltpu
from jax.sharding import PartitionSpec as P

B = 64
KA = 8
KP = 4
A3G = 12
TR = 4
ALL = ("grp", "row")


def passed_along(array, by):
    devices = lax.axis_size(ALL)
    pairs = [(i, i + by) for i in range(devices) if 0 <= i + by < devices]
    return lax.ppermute(array, ALL, pairs)


def w_kernel(loc_ref, col_ref, a_ref, p_ref, out_ref, *accs):
    step = pl.program_id(0)
    lane = lax.broadcasted_iota(jnp.int32, (B, 2 * B), 1)
    low = lane < B
    half = jnp.where(low, 0, 1)
    for r in range(TR):
        accs[r][...] = jnp.zeros_like(accs[r])
    for k in range(KA):
        for r in range(TR):
            acc = accs[r]
            j = loc_ref[(step * TR + r) * KA + k]
            block = p_ref[pl.ds(pl.multiple_of(j * B, B), B), :]
            prod = jnp.dot(
                a_ref[r * B : (r + 1) * B, k * B : (k + 1) * B],
                block,
                preferred_element_type=jnp.float32,
            )
            for c in range(KP // 2):
                x = prod[:, 2 * c * B : 2 * (c + 1) * B]
                turned = pltpu.roll(x, B, 1)
                pair = (jnp.where(low, x, turned), jnp.where(low, turned, x))
                for e in range(2):
                    t = col_ref[j * KP + 2 * c + e]
                    u = lax.shift_right_logical(t, 1)
                    h = lax.bitwise_and(t, 1)
                    acc[u] = acc[u] + jnp.where(half == h, pair[e], 0.0)
    for r in range(TR):
        for u in range(accs[r].shape[0]):
            out_ref[r * B : (r + 1) * B, 2 * u * B : 2 * (u + 1) * B] = accs[r][u].astype(
                jnp.bfloat16
            )


def w_rows(a, local, cols, ext_p, width):
    rows = a.shape[0]
    steps = rows // (TR * B)
    return pl.pallas_call(
        w_kernel,
        out_shape=jax.ShapeDtypeStruct((rows, width), jnp.bfloat16),
        grid_spec=pltpu.PrefetchScalarGridSpec(
            num_scalar_prefetch=2,
            grid=(steps,),
            in_specs=[
                pl.BlockSpec((TR * B, KA * B), lambda i, *_: (i, 0)),
                pl.BlockSpec(ext_p.shape, lambda i, *_: (0, 0)),
            ],
            out_specs=pl.BlockSpec((TR * B, width), lambda i, *_: (i, 0)),
            scratch_shapes=[pltpu.VMEM((width // (2 * B), B, 2 * B), jnp.float32)] * TR,
        ),
        compiler_params=pltpu.CompilerParams(vmem_limit_bytes=40 * 1024 * 1024),
        cost_estimate=pl.CostEstimate(
            flops=2 * rows * KA * B * KP * B,
            bytes_accessed=2 * (a.size + ext_p.size + rows * width),
            transcendentals=0,
        ),
    )(local, cols, a, ext_p)


def per_device(a_blocks, a_cols, a_count, p_blocks, p_cols, q2_blocks, agg3):
    rows_dev = a_cols.shape[0]
    coarse_dev = q2_blocks.shape[0]
    band = coarse_dev * B
    device = lax.axis_index(ALL)
    row_size = lax.axis_size("row")
    group = device // row_size
    f32, bf16 = jnp.float32, jnp.bfloat16

    near_cols = (p_cols - device * coarse_dev).reshape(-1)
    near_agg = agg3 - group * A3G
    ints = jnp.concatenate([near_agg, near_cols])
    ints = jnp.pad(ints, (0, B * B - ints.shape[0])).astype(bf16)[None, :]
    bundle = jnp.concatenate([q2_blocks, ints], axis=0)
    bundles = [passed_along(bundle, by) for by in (2, 1)]
    bundles += [bundle] + [passed_along(bundle, by) for by in (-1, -2)]
    p_before = passed_along(p_blocks, 1)
    p_after = passed_along(p_blocks, -1)
    ext_ints = jnp.stack([part[coarse_dev, : coarse_dev + rows_dev * KP] for part in bundles])
    ext_ints = ext_ints.astype(jnp.int32)
    steps = jnp.arange(5, dtype=jnp.int32)[:, None]
    ext_agg = ext_ints[:, :coarse_dev] + (device + steps - 2) // row_size * A3G
    ext_agg = ext_agg.reshape(-1)
    ext_cols = ext_ints[1:4, coarse_dev:] + steps[:3] * coarse_dev
    ext_cols = ext_cols.reshape(-1)

    keep = jnp.arange(KA * B, dtype=jnp.int32)[None, :] < (a_count * B)[:, None]
    amat = jnp.where(keep[:, None, :], a_blocks.reshape(rows_dev, B, KA * B), 0).astype(bf16)
    amat = amat.reshape(rows_dev * B, KA * B)
    local = (a_cols - (device - 1) * rows_dev).reshape(-1)
    p_turned = p_blocks.T.reshape(KP, 1, B, rows_dev * B)
    own_t = jnp.repeat((p_cols - device * coarse_dev).T, B, axis=1)
    t_ids = jnp.arange(2 * coarse_dev, dtype=jnp.int32)[:, None, None]
    p_dense = jnp.zeros((2 * coarse_dev, B, rows_dev * B), bf16)
    for m in range(KP):
        p_dense = jnp.where(own_t[m][None, None, :] == t_ids, p_turned[m], p_dense)
    p_dense = p_dense.reshape(2 * band, rows_dev * B)

    ext_q = jnp.concatenate([part[:coarse_dev] for part in bundles], axis=0)
    ext_q = ext_q.reshape(5 * band, B)
    slot = jnp.arange(2 * A3G * B, dtype=jnp.int32) // B
    lanes = (jnp.arange(2 * A3G * B, dtype=jnp.int32) % B)[None, :]
    spread = (jnp.arange(B, dtype=jnp.int32)[:, None] == lanes).astype(bf16)
    wide_q = jnp.dot(ext_q, spread, preferred_element_type=f32).astype(bf16)
    at = ext_agg - group * A3G
    outside = (at < 0) | (at >= A3G)
    at = jnp.where(outside, A3G + jnp.where(at < 0, at + A3G, at - A3G), at)
    at = jnp.repeat(at, B)
    window = jnp.where(at[:, None] == slot[None, :], wide_q, 0).astype(bf16)
    local, amat, p_dense, window = lax.optimization_barrier((local, amat, p_dense, window))
    ext_p = jnp.concatenate([p_before, p_blocks, p_after], axis=0)
    w = w_rows(amat, local, ext_cols, ext_p, 4 * band)
    part = jnp.dot(p_dense[band:], w, preferred_element_type=f32).astype(bf16)
    sent = passed_along(part, 1)
    own = jnp.dot(p_dense[:band], w, preferred_element_type=f32)
    own = lax.optimization_barrier(own)
    level2 = jnp.pad(own, ((0, 0), (band, 0))) + jnp.pad(sent.astype(f32), ((0, 0), (0, band)))
    coarse = level2.astype(bf16)

    v = jnp.dot(coarse, window, preferred_element_type=f32).astype(bf16)
    own_q = window[2 * band : 3 * band, : A3G * B]
    share = lax.dot_general(own_q, v, (((0,), (0,)), ((), ())), preferred_element_type=f32)

    pieces = share.astype(bf16).reshape(row_size, A3G * B // row_size, 2 * A3G * B)
    pieces = lax.all_to_all(pieces, "row", 0, 0).astype(f32)
    middle = jnp.sum(pieces[:, :, : A3G * B], axis=0)
    before = pieces[0, :, A3G * B :] + pieces[1, :, A3G * B :]
    after = pieces[-2, :, A3G * B :] + pieces[-1, :, A3G * B :]
    summed = jnp.concatenate([before, middle, after], axis=1).astype(bf16)
    level3 = lax.all_gather(summed, "row", axis=0, tiled=True).astype(f32)
    return (coarse, level3)


def solution(mesh):
    in_specs = (
        P(ALL, None),
        P(ALL, None),
        P(ALL),
        P(ALL, None),
        P(ALL, None),
        P(ALL, None),
        P(ALL),
    )
    out_specs = (P(ALL, None), P("grp", None))
    return jax.shard_map(
        per_device, mesh=mesh, in_specs=in_specs, out_specs=out_specs, check_vma=False
    )
```

time: 1160 us -> 353 us (0.30)
  matrix products: 466 us -> 43.6 us
  local copies, waits for them, and re-layouts: 201 us -> 14.8 us
  starting transfers between devices: 170 us -> 23.8 us
  waiting for transfers between devices: 292 us -> 154 us
  blocking collectives: 0 us -> 58.1 us
  Pallas kernels: 0 us -> 16.6 us
  other arithmetic: 11.6 us -> 27 us
    dot_general x44 -> x4, matrix products: 466 us -> 43.6 us  [the longest x1 15.7 us: per_device(): lax.dot_general(own_q, v, (((0,), (0,)), ((), ())), preferred_element_typ...]
    psum x1 -> x0, waiting for transfers between devices: 241 us -> none  [per_device(): level3 = lax.psum(share_sum, 'row')]
    ppermute x13 -> x7, starting transfers between devices: 170 us -> 23.7 us  [passed_along(): return lax.ppermute(array, ALL, pairs)]
    reshape x26 -> x4, local copies, waits for them, and re-layouts: 78.1 us -> 2.05 us  [the longest x1 1.76 us: per_device(): ext_q = ext_q.reshape(5 * band, B)]
    all_gather x0 -> x1, waiting for transfers between devices: none -> 63.3 us  [per_device(): level3 = lax.all_gather(summed, 'row', axis=0, tiled=True).astype(f32)]
    all_to_all x0 -> x1, blocking collectives: none -> 58.1 us  [per_device(): pieces = lax.all_to_all(pieces, 'row', 0, 0).astype(f32)]
    ppermute x13 -> x7, waiting for transfers between devices: 51.6 us -> 90.5 us  [passed_along(): return lax.ppermute(array, ALL, pairs)]
    gather x20 -> x0, local copies, waits for them, and re-layouts: 33 us -> none  [the longest x10 27.3 us: accumulate_block_entry(): prow = ext_p[local]]
  transfers between devices with their start and end apart: 14 -> 8, of which waited for: 8 -> 4; matrix products, arithmetic and copies ran while one was open for 1% -> 11% of each run, Pallas kernels for 0% -> 0%
where the time goes in v1:
time: 353 us; the launch traced here: 352 us
  waiting for transfers between devices  154 us (44%)
  blocking collectives  58.1 us (16%)
  matrix products  43.6 us (12%)
  other arithmetic  27 us (8%)
  starting transfers between devices  23.8 us (7%)
  Pallas kernels  16.6 us (5%)
  local copies, waits for them, and re-layouts  14.8 us (4%)
  between operations  14.3 us (4%)
    ppermute x7, waiting for transfers between devices, passed_along(): return lax.ppermute(array, ALL, pairs)  90.5 us
    all_gather x1, waiting for transfers between devices, per_device(): level3 = lax.all_gather(summed, 'row', axis=0, tiled=True).astype(f32)  63.3 us
    all_to_all x1, blocking collectives, per_device(): pieces = lax.all_to_all(pieces, 'row', 0, 0).astype(f32)  58.1 us
    ppermute x7, starting transfers between devices, passed_along(): return lax.ppermute(array, ALL, pairs)  23.7 us
    pallas_call x1, Pallas kernels, w_rows(): pl.pallas_call(w_kernel, out_shape=jax.ShapeDtypeStruct((rows, width), jn...  16.6 us
    dot_general x1, matrix products, per_device(): lax.dot_general(own_q, v, (((0,), (0,)), ((), ())), preferred_element_typ...  15.7 us
    dot_general x1, matrix products, per_device(): part = jnp.dot(p_dense[band:], w, preferred_element_type=f32).astype(bf16)  13 us
    dot_general x1, matrix products, per_device(): own = jnp.dot(p_dense[:band], w, preferred_element_type=f32)  8.6 us
  transfers between devices with their start and end apart: 8, of which 4 were waited for; matrix products, arithmetic and copies ran while one was open for 11% of the time, Pallas kernels for 0%

profile of v1, /device:TPU:0, one launch (start us, length us, event | category | flops | bytes accessed | tf_op | source)
XLA Modules:
  0.0 352.1 jit_solution(1516490723288647091)
XLA Ops:
  8.9 1.6 pad_maximum_fusion.2
  13.1 6.1 %collective-permute-start.1 = (bf16[11,4096]{1,0:T(8,128)(2,1)}, bf16[11,4096]{1,0:T(8,128)(2,1)}, u32[]{:S(2)}, u32[]{:S(2)}) collective-permute-start(bf16[11,4096]{1,0:T(8,128)(2,1)} %pad_maximum_fusion.2), channel_id=1, source_target_pairs={{0,1},{1,2},{2,3},{3,4},{4,5},{5,6},{6,7},{7,8},{8,9},{9,10},{10,1... | collective-permute-start | bytes 270344 | tf_op jit(solution)/shard_map/ppermute | solution.py:21
  19.2 4.6 %collective-permute-start = (bf16[11,4096]{1,0:T(8,128)(2,1)}, bf16[11,4096]{1,0:T(8,128)(2,1)}, u32[]{:S(2)}, u32[]{:S(2)}) collective-permute-start(bf16[11,4096]{1,0:T(8,128)(2,1)} %pad_maximum_fusion.2), channel_id=1, source_target_pairs={{0,2},{1,3},{2,4},{3,5},{4,6},{5,7},{6,8},{7,9},{8,10},{9,11},{10,... | collective-permute-start | bytes 270344 | tf_op jit(solution)/shard_map/ppermute | solution.py:21
  23.9 5.8 %collective-permute-start.4 = (bf16[2560,256]{1,0:T(8,128)(2,1)}, bf16[2560,256]{1,0:T(8,128)(2,1)}, u32[]{:S(2)}, u32[]{:S(2)}) collective-permute-start(bf16[2560,256]{1,0:T(8,128)(2,1)} %param.10), channel_id=1, source_target_pairs={{0,1},{1,2},{2,3},{3,4},{4,5},{5,6},{6,7},{7,8},{8,9},{9,10},{10,1... | collective-permute-start | bytes 3932168 | tf_op jit(solution)/shard_map/ppermute | solution.py:21
  31.9 2.3 fusion.22
  36.8 2.0 bitcast_select_fusion.a_ref
  38.8 5.5 %select_select_fusion = bf16[20,64,2560]{2,1,0:T(8,128)(2,1)} fusion(pred[20,2560]{1,0:T(8,128)(4,1)S(1)} %get-tuple-element.22, pred[20,2560]{1,0:T(8,128)(4,1)S(1)} %get-tuple-element.23, pred[20,2560]{1,0:T(8,128)(4,1)S(1)} %get-tuple-element.24, pred[20,2560]{1,0:T(8,128)(4,1)S(1)} %get-tuple-element.25, bf16[64,2560]{1,0:T(8,128)(2,1)S(1)} %copy.17, ...), kind=kLoop, calls=%fused_computation.3 | loop fusion | flops 13107200 | bytes 8069120 | tf_op jit(solution)/shard_map/jit(_where)/select_n | solution.py:117
  44.3 1.5 collective-permute-start.5
  48.4 4.9 %concatenate.19 = bf16[50,4096]{1,0:T(8,128)(2,1)S(1)} concatenate(bf16[10,4096]{1,0:T(8,128)(2,1)} %bitcast.26, bf16[10,4096]{1,0:T(8,128)(2,1)} %bitcast.27, bf16[10,4096]{1,0:T(8,128)(2,1)S(1)} %copy-done.3, bf16[10,4096]{1,0:T(8,128)(2,1)} %bitcast.28, bf16[10,4096]{1,0:T(8,128)(2,1)S(1)} %bitcast.35), dimensions={0} | concatenate | bytes 819200 | tf_op jit(solution)/shard_map/concatenate | solution.py:120
  53.3 1.8 reshape.252
  55.1 6.3 %compare_select_fusion = bf16[3200,1536]{1,0:T(8,128)(2,1)} fusion(bf16[3200,64]{1,0:T(8,128)(2,1)} %reshape.252, s32[1536]{0:T(1024)S(1)} %get-tuple-element.27, s32[3200]{0:T(1024)S(1)} %eq.126, s32[1536]{0:T(1024)S(1)} %get-tuple-element.26), kind=kOutput, calls=%fused_computation | convolution fusion | flops 643989504 | bytes 10265088 | tf_op jit(solution)/shard_map/dot_general | solution.py:125
  61.4 24.3 %collective-permute-done.4 = bf16[2560,256]{1,0:T(8,128)(2,1)} collective-permute-done((bf16[2560,256]{1,0:T(8,128)(2,1)}, bf16[2560,256]{1,0:T(8,128)(2,1)}, u32[]{:S(2)}, u32[]{:S(2)}) %collective-permute-start.4) | collective-permute-done | bytes 1310752 | tf_op jit(solution)/shard_map/ppermute | solution.py:21
  85.7 5.2 %collective-permute-done.5 = bf16[2560,256]{1,0:T(8,128)(2,1)} collective-permute-done((bf16[2560,256]{1,0:T(8,128)(2,1)}, bf16[2560,256]{1,0:T(8,128)(2,1)}, u32[]{:S(2)}, u32[]{:S(2)}) %collective-permute-start.5) | collective-permute-done | bytes 1310752 | tf_op jit(solution)/shard_map/ppermute | solution.py:21
  90.9 2.6 pad_maximum_fusion.p_ref
  93.5 16.6 %shard_map.86 = bf16[2560,2560]{1,0:T(8,128)(2,1)} custom-call(s32[320]{0:T(512)S(1)} %reshape.250.loc_ref, s32[480]{0:T(512)S(1)} %reshape.253.col_ref, bf16[2560,512]{1,0:T(8,128)(2,1)S(1)} %bitcast_select_fusion.a_ref, bf16[7680,256]{1,0:T(8,128)(2,1)S(1)} %pad_maximum_fusion.p_ref), custom_call_target="tpu_custom_call" | custom-call | flops 671088640 | bytes 19660800 | tf_op jit(solution)/shard_map/pallas_call | solution.py:60
  110.1 13.0 %convolution_convert_fusion.1 = bf16[640,2560]{1,0:T(8,128)(2,1)} fusion(bf16[2560,2560]{1,0:T(8,128)(2,1)} %shard_map.86, bf16[1280,2560]{1,0:T(8,128)(2,1)S(1)} %bitcast.32), kind=kOutput, calls=%fused_computation.5 | convolution fusion | flops 8390246400 | bytes 19660800 | tf_op jit(solution)/shard_map/dot_general | solution.py:134
  123.1 3.1 collective-permute-start.6
  126.2 8.6 %fusion.1 = f32[640,2560]{1,0:T(8,128)S(1)} fusion(bf16[2560,2560]{1,0:T(8,128)(2,1)S(1)} %copy-done, bf16[1280,2560]{1,0:T(8,128)(2,1)S(1)} %bitcast.33), kind=kOutput, calls=%fused_computation.9 | convolution fusion | flops 8388608000 | bytes 22937600 | tf_op jit(solution)/shard_map/dot_general | solution.py:136
  134.8 61.0 %collective-permute-done.6 = bf16[640,2560]{1,0:T(8,128)(2,1)} collective-permute-done((bf16[640,2560]{1,0:T(8,128)(2,1)}, bf16[640,2560]{1,0:T(8,128)(2,1)}, u32[]{:S(2)}, u32[]{:S(2)}) %collective-permute-start.6) | collective-permute-done | bytes 3276832 | tf_op jit(solution)/shard_map/ppermute | solution.py:21
  195.9 5.0 %add_convert_fusion = bf16[640,3200]{1,0:T(8,128)(2,1)} fusion(f32[640,2560]{1,0:T(8,128)S(1)} %fusion.1, bf16[640,2560]{1,0:T(8,128)(2,1)} %collective-permute-done.6), kind=kLoop, calls=%fused_computation.2 | loop fusion | flops 6144000 | bytes 13926400 | tf_op jit(solution)/shard_map/convert_element_type | solution.py:139
  200.9 15.7 %convolution_convert_fusion.2 = bf16[768,1536]{1,0:T(8,128)(2,1)S(1)} fusion(bf16[3200,1536]{1,0:T(8,128)(2,1)} %compare_select_fusion, bf16[640,3200]{1,0:T(8,128)(2,1)} %add_convert_fusion), kind=kOutput, calls=%fused_computation.7 | convolution fusion | flops 7803568128 | bytes 17268736 | tf_op jit(solution)/shard_map/dot_general | solution.py:143
  216.6 58.1 %all_to_all.5 = bf16[8,96,1536]{2,1,0:T(8,128)(2,1)S(1)} all-to-all(bf16[8,96,1536]{2,1,0:T(8,128)(2,1)S(1)} %bitcast.34), channel_id=1, replica_groups=mesh['grp'=4,'row'=8] {'row'}, dimensions={0} | all-to-all | bytes 4718592 | tf_op jit(solution)/shard_map/all_to_all | solution.py:146
  276.4 63.3 %all-gather.2.cloned.1.call-done = bf16[768,2304]{1,0:T(8,128)(2,1)} async-done(((bf16[96,2304]{1,0:T(8,128)(2,1)}), bf16[768,2304]{1,0:T(8,128)(2,1)}) %all-gather.2.cloned.1.call-update) | async-done | bytes 3538960 | tf_op jit(solution)/shard_map/all_gather | solution.py:151
  339.8 5.5 %convert_element_type.43 = f32[768,2304]{1,0:T(8,128)} convert(bf16[768,2304]{1,0:T(8,128)(2,1)} %all-gather.2.cloned.1.call-done) | non-fusion elementwise | flops 1769472 | bytes 10616832 | tf_op jit(solution)/shard_map/convert_element_type | solution.py:151
  (72 shorter events, 13.3 us)
Async XLA Ops:
  7.2 332.6 %all-gather.2.cloned.1.call-start = ((), (), s32[]{:S(2)}) async-start(), calls=%async_computation.1 | async-start | bytes 3981312 | tf_op jit(solution)/shard_map/all_gather | solution.py:151
  8.9 21.4 %copy-start.4 = (bf16[1,4096]{1,0:T(2,128)(2,1)}, bf16[1,4096]{1,0:T(2,128)(2,1)S(1)}, u32[]{:S(2)}) copy-start(bf16[1,4096]{1,0:T(2,128)(2,1)S(1)} %broadcast_in_dim.106) | copy-start | bytes 24580
  10.5 33.8 %collective-permute-start.3 = (bf16[11,4096]{1,0:T(8,128)(2,1)}, bf16[11,4096]{1,0:T(8,128)(2,1)S(1)}, u32[]{:S(2)}, u32[]{:S(2)}) collective-permute-start(bf16[11,4096]{1,0:T(8,128)(2,1)} %pad_maximum_fusion.2), channel_id=1, source_target_pairs={{2,0},{3,1},{4,2},{5,3},{6,4},{7,5},{8,6},{9,7},{10,8},{11,9},{12,... | collective-permute-start | bytes 270344 | tf_op jit(solution)/shard_map/ppermute | solution.py:21
  11.8 34.0 %collective-permute-start.2 = (bf16[11,4096]{1,0:T(8,128)(2,1)}, bf16[11,4096]{1,0:T(8,128)(2,1)}, u32[]{:S(2)}, u32[]{:S(2)}) collective-permute-start(bf16[11,4096]{1,0:T(8,128)(2,1)} %pad_maximum_fusion.2), channel_id=1, source_target_pairs={{1,0},{2,1},{3,2},{4,3},{5,4},{6,5},{7,6},{8,7},{9,8},{10,9},{11,1... | collective-permute-start | bytes 270344 | tf_op jit(solution)/shard_map/ppermute | solution.py:21
  13.1 33.4 %collective-permute-start.1 = (bf16[11,4096]{1,0:T(8,128)(2,1)}, bf16[11,4096]{1,0:T(8,128)(2,1)}, u32[]{:S(2)}, u32[]{:S(2)}) collective-permute-start(bf16[11,4096]{1,0:T(8,128)(2,1)} %pad_maximum_fusion.2), channel_id=1, source_target_pairs={{0,1},{1,2},{2,3},{3,4},{4,5},{5,6},{6,7},{7,8},{8,9},{9,10},{10,1... | collective-permute-start | bytes 270344 | tf_op jit(solution)/shard_map/ppermute | solution.py:21
  19.2 27.9 %collective-permute-start = (bf16[11,4096]{1,0:T(8,128)(2,1)}, bf16[11,4096]{1,0:T(8,128)(2,1)}, u32[]{:S(2)}, u32[]{:S(2)}) collective-permute-start(bf16[11,4096]{1,0:T(8,128)(2,1)} %pad_maximum_fusion.2), channel_id=1, source_target_pairs={{0,2},{1,3},{2,4},{3,5},{4,6},{5,7},{6,8},{7,9},{8,10},{9,11},{10,... | collective-permute-start | bytes 270344 | tf_op jit(solution)/shard_map/ppermute | solution.py:21
  23.9 61.8 %collective-permute-start.4 = (bf16[2560,256]{1,0:T(8,128)(2,1)}, bf16[2560,256]{1,0:T(8,128)(2,1)}, u32[]{:S(2)}, u32[]{:S(2)}) collective-permute-start(bf16[2560,256]{1,0:T(8,128)(2,1)} %param.10), channel_id=1, source_target_pairs={{0,1},{1,2},{2,3},{3,4},{4,5},{5,6},{6,7},{7,8},{8,9},{9,10},{10,1... | collective-permute-start | bytes 3932168 | tf_op jit(solution)/shard_map/ppermute | solution.py:21
  36.6 2.2 copy-start.1
  36.6 2.2 copy-start.2
  38.8 9.1 %slice-start.2 = ((bf16[1,4096]{1,0:T(2,128)(2,1)}), bf16[1,170]{1,0:T(2,128)(2,1)S(1)}, s32[]{:S(2)}) async-start(bf16[1,4096]{1,0:T(2,128)(2,1)} %copy-done.4), calls=%async_computation.4 | async-start | bytes 2048 | tf_op jit(solution)/shard_map/slice | solution.py:100
  38.8 9.6 %copy-start.3 = (bf16[10,4096]{1,0:T(8,128)(2,1)S(1)}, bf16[10,4096]{1,0:T(8,128)(2,1)}, u32[]{:S(2)}) copy-start(bf16[10,4096]{1,0:T(8,128)(2,1)} %param.12) | copy-start | bytes 245764
  44.3 46.6 %collective-permute-start.5 = (bf16[2560,256]{1,0:T(8,128)(2,1)}, bf16[2560,256]{1,0:T(8,128)(2,1)}, u32[]{:S(2)}, u32[]{:S(2)}) collective-permute-start(bf16[2560,256]{1,0:T(8,128)(2,1)} %param.10), channel_id=1, source_target_pairs={{1,0},{2,1},{3,2},{4,3},{5,4},{6,5},{7,6},{8,7},{9,8},{10,9},{11,1... | collective-permute-start | bytes 3932168 | tf_op jit(solution)/shard_map/ppermute | solution.py:21
  90.9 19.2 %slice-start = ((s8[6553600]{0:T(1024)(128)(4,1)}), s8[4194304]{0:T(1024)(128)(4,1)S(1)}, s32[]{:S(2)}) async-start(s8[6553600]{0:T(1024)(128)(4,1)} %bitcast.30), calls=%async_computation.2 | async-start | bytes 8388608
  93.5 16.6 %slice-start.1 = ((s8[6553600]{0:T(1024)(128)(4,1)}), s8[2359296]{0:T(1024)(128)(4,1)S(1)}, s32[]{:S(2)}) async-start(s8[6553600]{0:T(1024)(128)(4,1)} %bitcast.30), calls=%async_computation.3 | async-start | bytes 4718592
  110.1 16.1 %copy-start = (bf16[2560,2560]{1,0:T(8,128)(2,1)S(1)}, bf16[2560,2560]{1,0:T(8,128)(2,1)}, u32[]{:S(2)}) copy-start(bf16[2560,2560]{1,0:T(8,128)(2,1)} %shard_map.86) | copy-start | bytes 39321604
  123.1 72.8 %collective-permute-start.6 = (bf16[640,2560]{1,0:T(8,128)(2,1)}, bf16[640,2560]{1,0:T(8,128)(2,1)}, u32[]{:S(2)}, u32[]{:S(2)}) collective-permute-start(bf16[640,2560]{1,0:T(8,128)(2,1)} %convolution_convert_fusion.1), channel_id=1, source_target_pairs={{0,1},{1,2},{2,3},{3,4},{4,5},{5,6},{6,7},{7,8},{8,9},{9,10},{10,1... | collective-permute-start | bytes 9830408 | tf_op jit(solution)/shard_map/ppermute | solution.py:21
Sparse Core Ops, SparseCore 0:
  276.6 63.1 all-gather.1

commit v2 on v1

--- a/solution.py
+++ b/solution.py
@@ -88,26 +88,27 @@
     group = device // row_size
     f32, bf16 = jnp.float32, jnp.bfloat16
 
+    p_before = passed_along(p_blocks, 1)
+    p_after = passed_along(p_blocks, -1)
     near_cols = (p_cols - device * coarse_dev).reshape(-1)
     near_agg = agg3 - group * A3G
     ints = jnp.concatenate([near_agg, near_cols])
     ints = jnp.pad(ints, (0, B * B - ints.shape[0])).astype(bf16)[None, :]
     bundle = jnp.concatenate([q2_blocks, ints], axis=0)
-    bundles = [passed_along(bundle, by) for by in (2, 1)]
-    bundles += [bundle] + [passed_along(bundle, by) for by in (-1, -2)]
-    p_before = passed_along(p_blocks, 1)
-    p_after = passed_along(p_blocks, -1)
-    ext_ints = jnp.stack([part[coarse_dev, : coarse_dev + rows_dev * KP] for part in bundles])
-    ext_ints = ext_ints.astype(jnp.int32)
-    steps = jnp.arange(5, dtype=jnp.int32)[:, None]
-    ext_agg = ext_ints[:, :coarse_dev] + (device + steps - 2) // row_size * A3G
-    ext_agg = ext_agg.reshape(-1)
-    ext_cols = ext_ints[1:4, coarse_dev:] + steps[:3] * coarse_dev
-    ext_cols = ext_cols.reshape(-1)
-
     keep = jnp.arange(KA * B, dtype=jnp.int32)[None, :] < (a_count * B)[:, None]
     amat = jnp.where(keep[:, None, :], a_blocks.reshape(rows_dev, B, KA * B), 0).astype(bf16)
     amat = amat.reshape(rows_dev * B, KA * B)
+    bundles = [passed_along(bundle, 1), bundle, passed_along(bundle, -1)]
+    late, p_before = lax.optimization_barrier((bundle, p_before))
+    bundles = [passed_along(late, 2)] + bundles + [passed_along(late, -2)]
+    ext_ints = [part[coarse_dev, : coarse_dev + rows_dev * KP] for part in bundles]
+    steps = jnp.arange(5, dtype=jnp.int32)[:, None]
+    ext_agg = jnp.stack([x[:coarse_dev] for x in ext_ints]).astype(jnp.int32)
+    ext_agg = ext_agg + (device + steps - 2) // row_size * A3G
+    ext_agg = ext_agg.reshape(-1)
+    ext_cols = jnp.stack([x[coarse_dev:] for x in ext_ints[1:4]]).astype(jnp.int32)
+    ext_cols = ext_cols + steps[:3] * coarse_dev
+    ext_cols = ext_cols.reshape(-1)
     local = (a_cols - (device - 1) * rows_dev).reshape(-1)
     p_turned = p_blocks.T.reshape(KP, 1, B, rows_dev * B)
     own_t = jnp.repeat((p_cols - device * coarse_dev).T, B, axis=1)
@@ -128,13 +129,13 @@
     at = jnp.where(outside, A3G + jnp.where(at < 0, at + A3G, at - A3G), at)
     at = jnp.repeat(at, B)
     window = jnp.where(at[:, None] == slot[None, :], wide_q, 0).astype(bf16)
-    local, amat, p_dense, window = lax.optimization_barrier((local, amat, p_dense, window))
+    local, amat, p_dense = lax.optimization_barrier((local, amat, p_dense))
     ext_p = jnp.concatenate([p_before, p_blocks, p_after], axis=0)
     w = w_rows(amat, local, ext_cols, ext_p, 4 * band)
     part = jnp.dot(p_dense[band:], w, preferred_element_type=f32).astype(bf16)
     sent = passed_along(part, 1)
     own = jnp.dot(p_dense[:band], w, preferred_element_type=f32)
-    own = lax.optimization_barrier(own)
+    own, window = lax.optimization_barrier((own, window))
     level2 = jnp.pad(own, ((0, 0), (band, 0))) + jnp.pad(sent.astype(f32), ((0, 0), (0, band)))
     coarse = level2.astype(bf16)
 
@@ -142,13 +143,16 @@
     own_q = window[2 * band : 3 * band, : A3G * B]
     share = lax.dot_general(own_q, v, (((0,), (0,)), ((), ())), preferred_element_type=f32)
 
-    pieces = share.astype(bf16).reshape(row_size, A3G * B // row_size, 2 * A3G * B)
-    pieces = lax.all_to_all(pieces, "row", 0, 0).astype(f32)
-    middle = jnp.sum(pieces[:, :, : A3G * B], axis=0)
-    before = pieces[0, :, A3G * B :] + pieces[1, :, A3G * B :]
-    after = pieces[-2, :, A3G * B :] + pieces[-1, :, A3G * B :]
-    summed = jnp.concatenate([before, middle, after], axis=1).astype(bf16)
-    level3 = lax.all_gather(summed, "row", axis=0, tiled=True).astype(f32)
+    wide = A3G * B
+    share = share.astype(bf16).reshape(row_size, wide // row_size, 2 * wide)
+    far = lax.all_to_all(share[:, :, wide:], "row", 0, 0).astype(f32)
+    far = jnp.concatenate([far[0] + far[1], far[-2] + far[-1]], axis=1).astype(bf16)
+    far, mine = lax.optimization_barrier((far, share[:, :, :wide]))
+    far = lax.all_gather(far, "row", axis=0, tiled=True)
+    mine = lax.all_to_all(mine, "row", 0, 0).astype(f32)
+    mine = jnp.sum(mine, axis=0).astype(bf16)
+    mine = lax.all_gather(mine, "row", axis=0, tiled=True)
+    level3 = jnp.concatenate([far[:, :wide], mine, far[:, wide:]], axis=1).astype(f32)
     return (coarse, level3)
 
 

time: 353 us -> 370 us (1.048)
  blocking collectives: 58.1 us -> 96.9 us
  waiting for transfers between devices: 154 us -> 143 us
  local copies, waits for them, and re-layouts: 14.8 us -> 9.43 us
  starting transfers between devices: 23.8 us -> 19.2 us
    all_to_all x1 -> x2, blocking collectives: 58.1 us -> 96.9 us  [the longest x1 49 us: per_device(): far = lax.all_to_all(share[:, :, wide:], 'row', 0, 0).astype(f32)]
    all_gather x1 -> x2, waiting for transfers between devices: 63.3 us -> 54.1 us  [the longest x1 39.7 us: per_device(): mine = lax.all_gather(mine, 'row', axis=0, tiled=True)]
    ppermute x7, starting transfers between devices: 23.7 us -> 19.1 us  [passed_along(): return lax.ppermute(array, ALL, pairs)]
    concatenate x1, local copies, waits for them, and re-layouts: 4.94 us -> 0.93 us  [per_device(): ext_q = jnp.concatenate([part[:coarse_dev] for part in bundles], axis=0)]
  transfers between devices with their start and end apart: 8 -> 9, of which waited for: 4 -> 5; matrix products, arithmetic and copies ran while one was open for 11% -> 10% of each run, Pallas kernels for 0% -> 0%
where the time goes in v2:
time: 370 us; the launch traced here: 369 us
  waiting for transfers between devices  143 us (39%)
  blocking collectives  96.9 us (26%)
  matrix products  45.7 us (12%)
  other arithmetic  23.7 us (6%)
  starting transfers between devices  19.2 us (5%)
  Pallas kernels  16.6 us (4%)
  between operations  14.4 us (4%)
  local copies, waits for them, and re-layouts  9.43 us (3%)
    ppermute x7, waiting for transfers between devices, passed_along(): return lax.ppermute(array, ALL, pairs)  89.4 us
    all_to_all x1, blocking collectives, per_device(): far = lax.all_to_all(share[:, :, wide:], 'row', 0, 0).astype(f32)  49 us
    all_to_all x1, blocking collectives, per_device(): mine = lax.all_to_all(mine, 'row', 0, 0).astype(f32)  47.9 us
    all_gather x1, waiting for transfers between devices, per_device(): mine = lax.all_gather(mine, 'row', axis=0, tiled=True)  39.7 us
    ppermute x7, starting transfers between devices, passed_along(): return lax.ppermute(array, ALL, pairs)  19.1 us
    pallas_call x1, Pallas kernels, w_rows(): pl.pallas_call(w_kernel, out_shape=jax.ShapeDtypeStruct((rows, width), jn...  16.6 us
    dot_general x1, matrix products, per_device(): lax.dot_general(own_q, v, (((0,), (0,)), ((), ())), preferred_element_typ...  15.7 us
    all_gather x1, waiting for transfers between devices, per_device(): far = lax.all_gather(far, 'row', axis=0, tiled=True)  14.4 us
  transfers between devices with their start and end apart: 9, of which 5 were waited for; matrix products, arithmetic and copies ran while one was open for 10% of the time, Pallas kernels for 0%

profile of v2, /device:TPU:0, one launch (start us, length us, event | category | flops | bytes accessed | tf_op | source)
XLA Modules:
  0.0 369.2 jit_solution(10335925056940779259)
XLA Ops:
  7.2 5.9 %collective-permute-start.2 = (bf16[2560,256]{1,0:T(8,128)(2,1)}, bf16[2560,256]{1,0:T(8,128)(2,1)}, u32[]{:S(2)}, u32[]{:S(2)}) collective-permute-start(bf16[2560,256]{1,0:T(8,128)(2,1)} %param.10), channel_id=1, source_target_pairs={{0,1},{1,2},{2,3},{3,4},{4,5},{5,6},{6,7},{7,8},{8,9},{9,10},{10,1... | collective-permute-start | bytes 3932168 | tf_op jit(solution)/shard_map/ppermute | solution.py:21
  17.1 4.6 %collective-permute-start = (bf16[11,4096]{1,0:T(8,128)(2,1)S(1)}, bf16[11,4096]{1,0:T(8,128)(2,1)S(1)}, u32[]{:S(2)}, u32[]{:S(2)}) collective-permute-start(bf16[11,4096]{1,0:T(8,128)(2,1)S(1)} %pad_maximum_fusion.2), channel_id=1, source_target_pairs={{0,1},{1,2},{2,3},{3,4},{4,5},{5,6},{6,7},{7,8},{8,9},{9,10},{10,1... | collective-permute-start | bytes 270344 | tf_op jit(solution)/shard_map/ppermute | solution.py:21
  23.6 2.2 fusion.23
  27.0 5.5 %select_select_fusion = bf16[20,64,2560]{2,1,0:T(8,128)(2,1)} fusion(pred[20,2560]{1,0:T(8,128)(4,1)S(1)} %get-tuple-element.36, pred[20,2560]{1,0:T(8,128)(4,1)S(1)} %get-tuple-element.37, pred[20,2560]{1,0:T(8,128)(4,1)S(1)} %get-tuple-element.38, pred[20,2560]{1,0:T(8,128)(4,1)S(1)} %get-tuple-element.39, bf16[64,2560]{1,0:T(8,128)(2,1)S(1)} %copy.17, ...), kind=kLoop, calls=%fused_computation.3 | loop fusion | flops 13107200 | bytes 8069120 | tf_op jit(solution)/shard_map/jit(_where)/select_n | solution.py:118
  32.7 2.0 bitcast_select_fusion.a_ref
  34.7 39.3 %collective-permute-done = bf16[11,4096]{1,0:T(8,128)(2,1)S(1)} collective-permute-done((bf16[11,4096]{1,0:T(8,128)(2,1)S(1)}, bf16[11,4096]{1,0:T(8,128)(2,1)S(1)}, u32[]{:S(2)}, u32[]{:S(2)}) %collective-permute-start) | collective-permute-done | bytes 90144 | tf_op jit(solution)/shard_map/ppermute | solution.py:21
  74.1 4.0 %collective-permute-done.1 = bf16[11,4096]{1,0:T(8,128)(2,1)S(1)} collective-permute-done((bf16[11,4096]{1,0:T(8,128)(2,1)S(1)}, bf16[11,4096]{1,0:T(8,128)(2,1)S(1)}, u32[]{:S(2)}, u32[]{:S(2)}) %collective-permute-start.1) | collective-permute-done | bytes 90144 | tf_op jit(solution)/shard_map/ppermute | solution.py:21
  78.4 2.6 pad_maximum_fusion.p_ref
  81.0 16.6 %shard_map.86 = bf16[2560,2560]{1,0:T(8,128)(2,1)} custom-call(s32[320]{0:T(512)S(1)} %reshape.272.loc_ref, s32[480]{0:T(512)S(1)} %add.99.col_ref, bf16[2560,512]{1,0:T(8,128)(2,1)S(1)} %bitcast_select_fusion.a_ref, bf16[7680,256]{1,0:T(8,128)(2,1)S(1)} %pad_maximum_fusion.p_ref), custom_call_target="tpu_custom_call" | custom-call | flops 671088640 | bytes 19660800 | tf_op jit(solution)/shard_map/pallas_call | solution.py:60
  97.5 13.0 %convolution_convert_fusion.1 = bf16[640,2560]{1,0:T(8,128)(2,1)} fusion(bf16[2560,2560]{1,0:T(8,128)(2,1)} %shard_map.86, bf16[1280,2560]{1,0:T(8,128)(2,1)S(1)} %bitcast.33), kind=kOutput, calls=%fused_computation.5 | convolution fusion | flops 8390246400 | bytes 19660800 | tf_op jit(solution)/shard_map/dot_general | solution.py:135
  110.5 3.1 collective-permute-start.6
  115.1 1.5 collective-permute-start.5
  116.6 10.5 %fusion.1 = f32[640,2560]{1,0:T(8,128)} fusion(bf16[2560,2560]{1,0:T(8,128)(2,1)S(1)} %copy-done, bf16[1280,2560]{1,0:T(8,128)(2,1)S(1)} %bitcast.34), kind=kOutput, calls=%fused_computation.10 | convolution fusion | flops 8388608000 | bytes 22937600 | tf_op jit(solution)/shard_map/dot_general | solution.py:137
  128.1 1.8 reshape.274
  130.3 6.5 %compare_select_fusion = bf16[3200,1536]{1,0:T(8,128)(2,1)} fusion(bf16[3200,64]{1,0:T(8,128)(2,1)} %reshape.274, s32[1536]{0:T(1024)S(1)} %get-tuple-element.41, s32[3200]{0:T(1024)S(1)} %eq.126, s32[1536]{0:T(1024)S(1)} %get-tuple-element.40), kind=kOutput, calls=%fused_computation | convolution fusion | flops 643989504 | bytes 10265088 | tf_op jit(solution)/shard_map/dot_general | solution.py:126
  136.8 46.0 %collective-permute-done.6 = bf16[640,2560]{1,0:T(8,128)(2,1)} collective-permute-done((bf16[640,2560]{1,0:T(8,128)(2,1)}, bf16[640,2560]{1,0:T(8,128)(2,1)}, u32[]{:S(2)}, u32[]{:S(2)}) %collective-permute-start.6) | collective-permute-done | bytes 3276832 | tf_op jit(solution)/shard_map/ppermute | solution.py:21
  182.8 4.8 %add_convert_fusion = bf16[640,3200]{1,0:T(8,128)(2,1)} fusion(f32[640,2560]{1,0:T(8,128)S(1)} %bitcast.36, bf16[640,2560]{1,0:T(8,128)(2,1)} %collective-permute-done.6), kind=kLoop, calls=%fused_computation.2 | loop fusion | flops 6144000 | bytes 13926400 | tf_op jit(solution)/shard_map/convert_element_type | solution.py:140
  187.6 15.7 %convolution_convert_fusion.2 = bf16[768,1536]{1,0:T(8,128)(2,1)S(1)} fusion(bf16[3200,1536]{1,0:T(8,128)(2,1)} %compare_select_fusion, bf16[640,3200]{1,0:T(8,128)(2,1)} %add_convert_fusion), kind=kOutput, calls=%fused_computation.8 | convolution fusion | flops 7803568128 | bytes 17268736 | tf_op jit(solution)/shard_map/dot_general | solution.py:144
  203.4 49.0 %all_to_all.10 = bf16[8,96,768]{2,1,0:T(8,128)(2,1)S(1)} all-to-all(bf16[8,96,768]{2,1,0:T(8,128)(2,1)S(1)} %get-tuple-element.23), channel_id=1, replica_groups=mesh['grp'=4,'row'=8] {'row'}, dimensions={0} | all-to-all | bytes 2359296 | tf_op jit(solution)/shard_map/all_to_all | solution.py:148
  253.5 47.9 %all_to_all.11 = bf16[8,96,768]{2,1,0:T(8,128)(2,1)S(1)} all-to-all(bf16[8,96,768]{2,1,0:T(8,128)(2,1)S(1)} %get-tuple-element.19), channel_id=1, replica_groups=mesh['grp'=4,'row'=8] {'row'}, dimensions={0} | all-to-all | bytes 2359296 | tf_op jit(solution)/shard_map/all_to_all | solution.py:152
  302.3 14.4 %all-gather.3.cloned.1.call-done = bf16[768,1536]{1,0:T(8,128)(2,1)} async-done(((bf16[96,1536]{1,0:T(8,128)(2,1)}), bf16[768,1536]{1,0:T(8,128)(2,1)}) %all-gather.3.cloned.1.call-update) | async-done | bytes 2359312 | tf_op jit(solution)/shard_map/all_gather | solution.py:151
  316.7 1.8 fusion.21
  318.4 39.7 %all-gather.5.cloned.1.call-done = bf16[768,768]{1,0:T(8,128)(2,1)} async-done(((bf16[96,768]{1,0:T(8,128)(2,1)}), bf16[768,768]{1,0:T(8,128)(2,1)}) %all-gather.5.cloned.1.call-update) | async-done | bytes 1179664 | tf_op jit(solution)/shard_map/all_gather | solution.py:154
  358.1 4.3 %maximum_convert_fusion = f32[768,2304]{1,0:T(8,128)} fusion(bf16[768,768]{1,0:T(8,128)(2,1)S(1)} %get-tuple-element.21, bf16[768,768]{1,0:T(8,128)(2,1)} %all-gather.5.cloned.1.call-done, bf16[768,768]{1,0:T(8,128)(2,1)S(1)} %get-tuple-element.20), kind=kLoop, calls=%fused_computation.7 | loop fusion | flops 10616832 | bytes 10616832 | tf_op jit(solution)/shard_map/convert_element_type | solution.py:155
  (85 shorter events, 12.4 us)
Async XLA Ops:
  7.2 309.5 %all-gather.3.cloned.1.call-start = ((), (), s32[]{:S(2)}) async-start(), calls=%async_computation.2 | async-start | bytes 2654208 | tf_op jit(solution)/shard_map/all_gather | solution.py:151
  7.2 71.1 %collective-permute-start.2 = (bf16[2560,256]{1,0:T(8,128)(2,1)}, bf16[2560,256]{1,0:T(8,128)(2,1)}, u32[]{:S(2)}, u32[]{:S(2)}) collective-permute-start(bf16[2560,256]{1,0:T(8,128)(2,1)} %param.10), channel_id=1, source_target_pairs={{0,1},{1,2},{2,3},{3,4},{4,5},{5,6},{6,7},{7,8},{8,9},{9,10},{10,1... | collective-permute-start | bytes 3932168 | tf_op jit(solution)/shard_map/ppermute | solution.py:21
  13.1 65.2 %collective-permute-start.3 = (bf16[2560,256]{1,0:T(8,128)(2,1)}, bf16[2560,256]{1,0:T(8,128)(2,1)}, u32[]{:S(2)}, u32[]{:S(2)}) collective-permute-start(bf16[2560,256]{1,0:T(8,128)(2,1)} %param.10), channel_id=1, source_target_pairs={{1,0},{2,1},{3,2},{4,3},{5,4},{6,5},{7,6},{8,7},{9,8},{10,9},{11,1... | collective-permute-start | bytes 3932168 | tf_op jit(solution)/shard_map/ppermute | solution.py:21
  16.1 97.5 %copy-start.2 = (bf16[1,4096]{1,0:T(2,128)(2,1)}, bf16[1,4096]{1,0:T(2,128)(2,1)S(1)}, u32[]{:S(2)}) copy-start(bf16[1,4096]{1,0:T(2,128)(2,1)S(1)} %broadcast_in_dim.106) | copy-start | bytes 24580
  17.1 56.9 %collective-permute-start = (bf16[11,4096]{1,0:T(8,128)(2,1)S(1)}, bf16[11,4096]{1,0:T(8,128)(2,1)S(1)}, u32[]{:S(2)}, u32[]{:S(2)}) collective-permute-start(bf16[11,4096]{1,0:T(8,128)(2,1)S(1)} %pad_maximum_fusion.2), channel_id=1, source_target_pairs={{0,1},{1,2},{2,3},{3,4},{4,5},{5,6},{6,7},{7,8},{8,9},{9,10},{10,1... | collective-permute-start | bytes 270344 | tf_op jit(solution)/shard_map/ppermute | solution.py:21
  21.7 56.5 %collective-permute-start.1 = (bf16[11,4096]{1,0:T(8,128)(2,1)S(1)}, bf16[11,4096]{1,0:T(8,128)(2,1)S(1)}, u32[]{:S(2)}, u32[]{:S(2)}) collective-permute-start(bf16[11,4096]{1,0:T(8,128)(2,1)S(1)} %pad_maximum_fusion.2), channel_id=1, source_target_pairs={{1,0},{2,1},{3,2},{4,3},{5,4},{6,5},{7,6},{8,7},{9,8},{10,9},{11,1... | collective-permute-start | bytes 270344 | tf_op jit(solution)/shard_map/ppermute | solution.py:21
  23.5 3.2 copy-start.4
  23.6 3.5 copy-start.3
  78.4 19.2 %slice-start = ((s8[6553600]{0:T(1024)(128)(4,1)}), s8[4194304]{0:T(1024)(128)(4,1)S(1)}, s32[]{:S(2)}) async-start(s8[6553600]{0:T(1024)(128)(4,1)} %bitcast.31), calls=%async_computation.4 | async-start | bytes 8388608
  81.0 16.6 %slice-start.1 = ((s8[6553600]{0:T(1024)(128)(4,1)}), s8[2359296]{0:T(1024)(128)(4,1)S(1)}, s32[]{:S(2)}) async-start(s8[6553600]{0:T(1024)(128)(4,1)} %bitcast.31), calls=%async_computation.5 | async-start | bytes 4718592
  97.5 19.1 %copy-start = (bf16[2560,2560]{1,0:T(8,128)(2,1)S(1)}, bf16[2560,2560]{1,0:T(8,128)(2,1)}, u32[]{:S(2)}) copy-start(bf16[2560,2560]{1,0:T(8,128)(2,1)} %shard_map.86) | copy-start | bytes 39321604
  110.5 72.2 %collective-permute-start.6 = (bf16[640,2560]{1,0:T(8,128)(2,1)}, bf16[640,2560]{1,0:T(8,128)(2,1)}, u32[]{:S(2)}, u32[]{:S(2)}) collective-permute-start(bf16[640,2560]{1,0:T(8,128)(2,1)} %convolution_convert_fusion.1), channel_id=1, source_target_pairs={{0,1},{1,2},{2,3},{3,4},{4,5},{5,6},{6,7},{7,8},{8,9},{9,10},{10,1... | collective-permute-start | bytes 9830408 | tf_op jit(solution)/shard_map/ppermute | solution.py:21
  113.7 13.5 %copy-start.1 = (bf16[10,4096]{1,0:T(8,128)(2,1)S(1)}, bf16[10,4096]{1,0:T(8,128)(2,1)}, u32[]{:S(2)}) copy-start(bf16[10,4096]{1,0:T(8,128)(2,1)} %param.12) | copy-start | bytes 245764
  113.7 16.2 %slice-start.4 = ((bf16[1,4096]{1,0:T(2,128)(2,1)}), bf16[1,10]{1,0:T(2,128)(2,1)S(1)}, s32[]{:S(2)}) async-start(bf16[1,4096]{1,0:T(2,128)(2,1)} %copy-done.2), calls=%async_computation.8 | async-start | bytes 1024 | tf_op jit(solution)/shard_map/slice | solution.py:106
  113.7 13.5 %collective-permute-start.4 = (bf16[11,4096]{1,0:T(8,128)(2,1)S(1)}, bf16[11,4096]{1,0:T(8,128)(2,1)S(1)}, u32[]{:S(2)}, u32[]{:S(2)}) collective-permute-start(bf16[11,4096]{1,0:T(8,128)(2,1)S(1)} %pad_maximum_fusion.2), channel_id=1, source_target_pairs={{0,2},{1,3},{2,4},{3,5},{4,6},{5,7},{6,8},{7,9},{8,10},{9,11},{10,... | collective-permute-start | bytes 270344 | tf_op jit(solution)/shard_map/ppermute | solution.py:21
  115.1 12.0 %collective-permute-start.5 = (bf16[11,4096]{1,0:T(8,128)(2,1)S(1)}, bf16[11,4096]{1,0:T(8,128)(2,1)S(1)}, u32[]{:S(2)}, u32[]{:S(2)}) collective-permute-start(bf16[11,4096]{1,0:T(8,128)(2,1)S(1)} %pad_maximum_fusion.2), channel_id=1, source_target_pairs={{2,0},{3,1},{4,2},{5,3},{6,4},{7,5},{8,6},{9,7},{10,8},{11,9},{12,... | collective-permute-start | bytes 270344 | tf_op jit(solution)/shard_map/ppermute | solution.py:21
  128.1 54.6 %slice-start.2 = ((s8[6553600]{0:T(1024)(128)(4,1)}), s8[2359296]{0:T(1024)(128)(4,1)S(1)}, s32[]{:S(2)}) async-start(s8[6553600]{0:T(1024)(128)(4,1)} %bitcast.35), calls=%async_computation.6 | async-start | bytes 4718592
  130.3 52.5 %slice-start.3 = ((s8[6553600]{0:T(1024)(128)(4,1)}), s8[4194304]{0:T(1024)(128)(4,1)S(1)}, s32[]{:S(2)}) async-start(s8[6553600]{0:T(1024)(128)(4,1)} %bitcast.35), calls=%async_computation.7 | async-start | bytes 8388608
  253.4 104.7 %all-gather.5.cloned.1.call-start = ((), (), s32[]{:S(2)}) async-start(), calls=%async_computation.3 | async-start | bytes 1327104 | tf_op jit(solution)/shard_map/all_gather | solution.py:154
Sparse Core Ops, SparseCore 0:
  253.6 63.0 all-gather.2
  318.8 39.2 all-gather.4
